TPU v7x, 512 devices: a whole 4x4x16 slice. The times are simulated.
512 devices in a mesh: ctx: 64 (over z, x), head: 8 (over y, core).
Axes of the slice: x: 4, y: 4, z: 16, core: 2. Of those that a mesh axis runs over, the one named last changes fastest.
Arguments:
- queries: float32 [32768, 2048], P('ctx', 'head'), may hold values from -1024 to 1024
- keys: float32 [32768, 128], P('ctx'), may hold values from -1024 to 1024
- values: float32 [32768, 128], P('ctx'), may hold values from -6 to 6
- cotangent: float32 [32768, 2048], P('ctx', 'head'), may hold values from -384 to 384
- source_ids: int32 [32768], P('ctx'), may hold values from 0 to 63
- source_weights: float32 [64], replicated, may hold values from 0.25 to 4
- q_feature: float32 [16, 128, 128], P('head'), may hold values from -4 to 4
- k_feature: float32 [128, 128], replicated, may hold values from -4 to 4
Outputs:
- grad_queries: float32 [32768, 2048], P('ctx', 'head')
- grad_keys: float32 [32768, 128], P(('ctx', 'head'))
- grad_values: float32 [32768, 128], P(('ctx', 'head'))
- grad_q_feature: float32 [16, 128, 128], P('head')
- grad_k_feature: float32 [128, 128], replicated
All inputs are finite; a program needn't handle non-finite values.
Results may differ from a plain program's by a relative error of at most 0.0015.
Values sent between devices are 32-bit elements; how exact they have to be, the bound alone decides.
A program may use at most 64 MiB of HBM per device.

v0:
```python
import jax
import jax.numpy as jnp
from jax import lax
from jax.sharding import PartitionSpec as P


def entering(value, axis, join, neutral, backward):
    count, mine = (lax.axis_size(axis), lax.axis_index(axis))
    pieces = jax.tree.map(lambda part: lax.all_gather(part, axis), value)
    if backward:
        pieces = jax.tree.map(lambda part: part[::-1], pieces)
        mine = count - 1 - mine
    total = jax.tree.map(
        lambda part, zero: jnp.full_like(part, 0) + jnp.asarray(zero, part.dtype), value, neutral
    )

    def turn(position, total):
        longer = join(total, jax.tree.map(lambda part: part[position], pieces))
        return jax.tree.map(lambda new, old: jnp.where(position < mine, new, old), longer, total)

    return lax.fori_loop(0, count - 1, turn, total)


def matmul(left, right):
    return jnp.dot(left, right, precision=lax.Precision.HIGHEST, preferred_element_type=jnp.float32)


def product(form, left, right):
    return jnp.einsum(
        form, left, right, precision=lax.Precision.HIGHEST, preferred_element_type=jnp.float32
    )


def feature_map(inputs, weight):
    logits = matmul(inputs, weight)
    upper = jax.nn.softmax(logits, axis=-1)
    lower = jax.nn.softmax(-logits, axis=-1)
    return (jnp.concatenate([upper, lower], axis=-1), upper, lower)


def feature_back(inputs, weight, upper, lower, grad_feat):
    half = upper.shape[-1]
    grad_upper = grad_feat[:, :half]
    grad_lower = grad_feat[:, half:]
    grad_logits = upper * (grad_upper - jnp.sum(upper * grad_upper, axis=-1, keepdims=True))
    grad_logits = grad_logits - lower * (
        grad_lower - jnp.sum(lower * grad_lower, axis=-1, keepdims=True)
    )
    return (matmul(grad_logits, weight.T), matmul(inputs.T, grad_logits))


def causal_mask(count):
    row_index = lax.broadcasted_iota(jnp.int32, (count, count), 0)
    col_index = lax.broadcasted_iota(jnp.int32, (count, count), 1)
    return (row_index >= col_index).astype(jnp.float32)


def add_pair(earlier, later):
    return (earlier[0] + later[0], earlier[1] + later[1])


def block_terms(query_c, key_c, value_c, scaled_c, prefix, prefix_tot):
    lower_mask = causal_mask(query_c.shape[1])
    scores = product("ncf,ndf->ncd", query_c, key_c) * lower_mask
    numerator = product("ncd,nde->nce", scores, value_c) + product("ncf,nfe->nce", query_c, prefix)
    normalizer = jnp.sum(scores, axis=2) + product("ncf,nf->nc", query_c, prefix_tot)
    output = numerator / normalizer[..., None]
    grad_numer = scaled_c / normalizer[..., None]
    grad_norm = -jnp.sum(scaled_c * output, axis=2) / normalizer
    grad_scores = (product("nce,nde->ncd", grad_numer, value_c) + grad_norm[..., None]) * lower_mask
    grad_query = (
        product("ncd,ndf->ncf", grad_scores, key_c)
        + product("nce,nfe->ncf", grad_numer, prefix)
        + grad_norm[..., None] * prefix_tot[:, None, :]
    )
    grad_key = product("ncd,ncf->ndf", grad_scores, query_c)
    grad_value = product("ncd,nce->nde", scores, grad_numer)
    carried = product("ncf,nce->nfe", query_c, grad_numer)
    carried_totals = product("nc,ncf->nf", grad_norm, query_c)
    return (grad_query, grad_key, grad_value, carried, carried_totals)


def on_device(queries, keys, values, cotangent, source_ids, source_weights, q_feature, k_feature):
    head_count = q_feature.shape[0]
    width = q_feature.shape[1]
    features = 2 * q_feature.shape[2]
    rows = queries.shape[0]
    piece = min(128, rows)
    pieces = rows // piece
    source_index = lax.broadcasted_iota(jnp.int32, (1, source_weights.shape[0]), 1)
    lookup = (source_ids[:, None] == source_index).astype(jnp.float32)
    weight = jnp.sum(lookup * source_weights[None, :], axis=1)
    key_feat, key_upper, key_lower = feature_map(keys, k_feature)
    key_c = key_feat.reshape(pieces, piece, features)
    value_c = values.reshape(pieces, piece, width)
    piece_state = product("ncf,nce->nfe", key_c, value_c)
    piece_tot = jnp.sum(key_c, axis=1)
    whole_local = (jnp.sum(piece_state, axis=0), jnp.sum(piece_tot, axis=0))
    whole_zero = (jnp.zeros((features, width), jnp.float32), jnp.zeros((features,), jnp.float32))
    earlier, earlier_totals = entering(
        (whole_local[0], whole_local[1]), "ctx", add_pair, whole_zero, False
    )
    prefix = jnp.cumsum(piece_state, axis=0) - piece_state + earlier[None]
    prefix_tot = jnp.cumsum(piece_tot, axis=0) - piece_tot + earlier_totals[None]
    grad_keyfeat = jnp.zeros(key_feat.shape, jnp.float32)
    grad_vals = jnp.zeros(values.shape, jnp.float32)
    piece_carried = jnp.zeros((pieces, features, width), jnp.float32)
    piece_carried_tot = jnp.zeros((pieces, features), jnp.float32)
    query_grads = []
    weight_grads = []
    for head in range(head_count):
        query_head = queries[:, head * width : (head + 1) * width]
        query_feat, query_upper, query_lower = feature_map(query_head, q_feature[head])
        scaled = cotangent[:, head * width : (head + 1) * width] * weight[:, None]
        grad_query, grad_key, grad_value, carried, carried_totals = block_terms(
            query_feat.reshape(pieces, piece, features),
            key_c,
            value_c,
            scaled.reshape(pieces, piece, width),
            prefix,
            prefix_tot,
        )
        grad_head, grad_weight = feature_back(
            query_head,
            q_feature[head],
            query_upper,
            query_lower,
            grad_query.reshape(rows, features),
        )
        query_grads.append(grad_head)
        weight_grads.append(grad_weight)
        grad_keyfeat = grad_keyfeat + grad_key.reshape(rows, features)
        grad_vals = grad_vals + grad_value.reshape(rows, width)
        piece_carried = piece_carried + carried
        piece_carried_tot = piece_carried_tot + carried_totals
    carried_all = jnp.sum(piece_carried, axis=0)
    carried_tot = jnp.sum(piece_carried_tot, axis=0)
    inner_later = carried_all[None] - jnp.cumsum(piece_carried, axis=0)
    inner_tot = carried_tot[None] - jnp.cumsum(piece_carried_tot, axis=0)
    grad_keyfeat = grad_keyfeat + (
        product("nce,nfe->ncf", value_c, inner_later) + inner_tot[:, None, :]
    ).reshape(rows, features)
    grad_vals = grad_vals + product("ncf,nfe->nce", key_c, inner_later).reshape(rows, width)
    later, later_tot = entering((carried_all, carried_tot), "ctx", add_pair, whole_zero, True)
    grad_keyfeat = grad_keyfeat + matmul(values, later.T) + later_tot[None, :]
    grad_vals = grad_vals + matmul(key_feat, later)
    grad_key_part, grad_kweight = feature_back(keys, k_feature, key_upper, key_lower, grad_keyfeat)
    grad_keys, grad_values = (
        lax.psum_scatter(grad_key_part, "head", scatter_dimension=0, tiled=True),
        lax.psum_scatter(grad_vals, "head", scatter_dimension=0, tiled=True),
    )
    grad_qweight = lax.psum(jnp.stack(weight_grads, axis=0), "ctx")
    grad_kweight = lax.psum(grad_kweight, ("ctx", "head"))
    return (
        jnp.concatenate(query_grads, axis=1),
        grad_keys,
        grad_values,
        grad_qweight,
        grad_kweight,
    )


def solution(mesh):
    placed = (
        P("ctx", "head"),
        P("ctx", None),
        P("ctx", None),
        P("ctx", "head"),
        P("ctx"),
        P(),
        P("head", None, None),
        P(),
    )
    return jax.shard_map(
        on_device,
        mesh=mesh,
        in_specs=placed,
        out_specs=(
            P("ctx", "head"),
            P(("ctx", "head"), None),
            P(("ctx", "head"), None),
            P("head", None, None),
            P(),
        ),
        check_vma=False,
    )
```

profile of v0, /device:TPU:2, one launch (start us, length us, event | category | flops | bytes accessed | tf_op | source)
XLA Modules:
  0.0 1215.9 jit_solution(13639607046449780209)
XLA Ops:
  7.2 1.5 fusion.97
  9.8 2.1 fusion.103
  12.8 1.2 slice_multiply_fusion.1
  14.9 87.9 %all-gather.4 = f32[64,1,256]{2,1,0:T(1,128)S(1)} all-gather(f32[1,1,256]{2,1,0:T(1,128)S(1)} %bitcast.226), channel_id=3, replica_groups=mesh['ctx'=64,'head'=8] {'ctx'}, dimensions={0}, use_global_device_ids=true | all-gather | bytes 66560 | tf_op jit(solution)/shard_map/all_gather | solution.py:9
  103.5 1.3 reshape.116
  106.6 1.8 fusion.102
  108.4 1.8 fusion.104
  110.2 62.4 %all-gather.9.cloned.1.call-done = f32[16384,128]{1,0:T(8,128)} async-done(((f32[256,128]{1,0:T(8,128)}), f32[16384,128]{1,0:T(8,128)}) %all-gather.9.cloned.1.call-update) | async-done | bytes 8388624 | tf_op jit(solution)/shard_map/all_gather | solution.py:9
  172.6 106.3 %while.32 = (s32[]{:T(128)}, f32[256,128]{1,0:T(8,128)S(1)}, f32[256]{0:T(256)S(1)}, s32[]{:T(128)}, f32[64,256,128]{2,1,0:T(8,128)}, /*index=5*/f32[64,256]{1,0:T(8,128)}, s32[]{:T(128)}, s32[]{:T(128)}) while((s32[]{:T(128)}, f32[256,128]{1,0:T(8,128)S(1)}, f32[256]{0:T(256)S(1)}, s32[]{:T(128)}, f32[64,256,128]{2,1,0:T(8,128)}, ...), condition=%wide.region_15.16_spmd.clone, body=%wide.region_14.15_spmd.clone.sunk | while | flops 99076 | bytes 398459 | solution.py:21
  280.5 2.1 fusion.105
  282.9 1.3 fusion
  284.2 1.0 fusion.19
  285.3 1.6 fusion.14
  286.8 1.1 fusion.39
  287.9 1.6 fusion.15
  290.7 80.2 %all-gather.5 = f32[64,1,256]{2,1,0:T(1,128)S(1)} all-gather(f32[1,1,256]{2,1,0:T(1,128)S(1)} %bitcast.225), channel_id=5, replica_groups=mesh['ctx'=64,'head'=8] {'ctx'}, dimensions={0}, use_global_device_ids=true | all-gather | bytes 66560 | tf_op jit(solution)/shard_map/all_gather | solution.py:9
  374.8 1.8 copy.214
  376.6 1.8 copy.215
  378.4 1.4 fusion.11
  381.2 1.6 fusion.6
  385.1 1.5 fusion.44
  386.6 1.1 reduce-window_subtract_fusion
  387.7 1.5 convolution_add_fusion.2
  389.3 1.4 fusion.4
  390.7 2.0 copy.209
  392.7 1.8 copy.213
  394.5 1.0 multiply_reduce_fusion.2
  395.6 1.1 multiply_subtract_fusion.1
  396.7 1.4 convolution_bitcast_fusion.2
  398.1 1.1 multiply_reduce_fusion.4
  399.2 1.1 multiply_subtract_fusion.2
  400.3 1.3 convolution_bitcast_fusion.3
  402.3 1.7 fusion.93
  404.0 1.0 fusion.27
  405.1 1.6 fusion.7
  406.8 27.8 %all-gather.11.cloned.1.call-done = f32[16384,128]{1,0:T(8,128)} async-done(((f32[256,128]{1,0:T(8,128)}), f32[16384,128]{1,0:T(8,128)}) %all-gather.11.cloned.1.call-update) | async-done | bytes 8388624 | tf_op jit(solution)/shard_map/all_gather | solution.py:9
  434.6 7.7 rev.6
  442.2 106.4 %while.33 = (s32[]{:T(128)}, f32[256,128]{1,0:T(8,128)S(1)}, f32[256]{0:T(256)S(1)}, s32[]{:T(128)}, f32[64,256,128]{2,1,0:T(8,128)}, /*index=5*/f32[64,256]{1,0:T(8,128)}, s32[]{:T(128)}, s32[]{:T(128)}) while((s32[]{:T(128)}, f32[256,128]{1,0:T(8,128)S(1)}, f32[256]{0:T(256)S(1)}, s32[]{:T(128)}, f32[64,256,128]{2,1,0:T(8,128)}, ...), condition=%wide.region_33.34_spmd.clone, body=%wide.region_32.33_spmd.clone.sunk | while | flops 99076 | bytes 398459 | solution.py:21
  449.8 0.9 add_select_fusion.10
  454.8 0.9 add_select_fusion.10
  458.2 0.9 add_select_fusion.10
  459.9 0.9 add_select_fusion.10
  461.6 0.9 add_select_fusion.10
  465.0 0.9 add_select_fusion.10
  466.7 0.9 add_select_fusion.10
  470.0 0.9 add_select_fusion.10
  471.7 0.9 add_select_fusion.10
  473.4 0.9 add_select_fusion.10
  475.1 0.9 add_select_fusion.10
  476.8 0.9 add_select_fusion.10
  478.5 0.9 add_select_fusion.10
  483.5 0.9 add_select_fusion.10
  492.0 0.9 add_select_fusion.10
  495.4 0.9 add_select_fusion.10
  549.5 1.0 convolution_bitcast_fusion.1
  550.8 1.7 convolution_add_fusion.5
  552.6 1.3 fusion.106
  554.7 1.0 copy.180
  555.7 138.0 %all-reduce.3.cloned.1.call-done = f32[2,128,128]{1,2,0:T(8,128)} async-done(((f32[2,128,128]{1,2,0:T(8,128)}), f32[2,128,128]{1,2,0:T(8,128)}) %all-reduce.3.cloned.1.call-update) | async-done | bytes 131088 | tf_op jit(solution)/shard_map/psum | solution.py:152
  693.8 1.7 copy.181
  695.4 440.1 %all-reduce.5.cloned.1.call-done = f32[128,128]{0,1:T(8,128)} async-done(((f32[128,128]{0,1:T(8,128)}), f32[128,128]{0,1:T(8,128)}) %all-reduce.5.cloned.1.call-update) | async-done | bytes 65552 | tf_op jit(solution)/shard_map/psum | solution.py:153
  1135.6 1.6 copy.182
  1137.1 31.7 %reduce-scatter.5.cloned.1.call-done = f32[64,128]{1,0:T(8,128)} async-done(((f32[512,128]{1,0:T(8,128)}), f32[64,128]{1,0:T(8,128)}) %reduce-scatter.5.cloned.1.call-update) | async-done | bytes 32784 | tf_op jit(solution)/shard_map/reduce_scatter | solution.py:150
  1168.8 40.2 %reduce-scatter.3.cloned.1.call-done = f32[64,128]{1,0:T(8,128)} async-done(((f32[512,128]{1,0:T(8,128)}), f32[64,128]{1,0:T(8,128)}) %reduce-scatter.3.cloned.1.call-update) | async-done | bytes 32784 | tf_op jit(solution)/shard_map/reduce_scatter | solution.py:149
  (457 shorter events, 213.1 us)
Async XLA Ops:
  7.2 2.6 copy-start
  7.2 98.1 %copy-start.12 = (f32[2,128,128]{2,1,0:T(8,128)S(1)}, f32[2,128,128]{2,1,0:T(8,128)}, u32[]{:S(2)}) copy-start(f32[2,128,128]{2,1,0:T(8,128)} %param.18) | copy-start | bytes 393220
  7.2 98.1 %copy-start.4 = (f32[512,256]{1,0:T(8,128)S(1)}, f32[512,256]{1,0:T(8,128)}, u32[]{:S(2)}) copy-start(f32[512,256]{1,0:T(8,128)} %param.12) | copy-start | bytes 1572868
  7.2 165.4 %all-gather.9.cloned.1.call-start = ((), (), s32[]{:S(2)}) async-start(), calls=%async_computation.6 | async-start | bytes 8519680 | tf_op jit(solution)/shard_map/all_gather | solution.py:9
  11.9 422.7 %all-gather.11.cloned.1.call-start = ((), (), s32[]{:S(2)}) async-start(), calls=%async_computation.7 | async-start | bytes 8519680 | tf_op jit(solution)/shard_map/all_gather | solution.py:9
  105.1 174.8 %copy-start.8 = (f32[4,128,128]{1,2,0:T(8,128)S(1)}, f32[4,128,128]{1,2,0:T(8,128)}, u32[]{:S(2)}) copy-start(f32[4,128,128]{1,2,0:T(8,128)} %copy.142) | copy-start | bytes 786436
  105.3 173.6 %copy-start.10 = (f32[128,128]{0,1:T(8,128)}, f32[128,128]{0,1:T(8,128)S(1)}, u32[]{:S(2)}) copy-start(f32[128,128]{0,1:T(8,128)S(1)} %fusion.88) | copy-start | bytes 196612
  279.0 92.5 %copy-start.11 = (f32[128,128]{0,1:T(8,128)S(1)}, f32[128,128]{0,1:T(8,128)}, u32[]{:S(2)}) copy-start(f32[128,128]{0,1:T(8,128)} %copy-done.10) | copy-start | bytes 196612
  282.6 411.2 %all-reduce.3.cloned.1.call-start = ((), (), s32[]{:S(2)}) async-start(), calls=%async_computation.4 | async-start | bytes 262144 | tf_op jit(solution)/shard_map/psum | solution.py:152
  290.6 90.5 %copy-start.15 = (f32[256]{0:T(256)}, f32[256]{0:T(256)S(1)}, u32[]{:S(2)}) copy-start(f32[256]{0:T(256)S(1)} %get-tuple-element.329) | copy-start | bytes 3076
  372.0 0.7 copy-start.6
  379.8 0.7 copy-start.7
  382.8 11.8 copy-start.3
  396.6 3.7 copy-start.1
  406.7 728.8 %all-reduce.5.cloned.1.call-start = ((), (), s32[]{:S(2)}) async-start(), calls=%async_computation.5 | async-start | bytes 131072 | tf_op jit(solution)/shard_map/psum | solution.py:153
  434.6 114.1 %copy-start.5 = (f32[512,256]{0,1:T(8,128)S(1)}, f32[512,256]{0,1:T(8,128)}, u32[]{:S(2)}) copy-start(f32[512,256]{0,1:T(8,128)} %copy.209) | copy-start | bytes 1572868
  434.6 114.9 %copy-start.9 = (f32[512,128]{1,0:T(8,128)S(1)}, f32[512,128]{1,0:T(8,128)}, u32[]{:S(2)}) copy-start(f32[512,128]{1,0:T(8,128)} %param.13) | copy-start | bytes 786436
  434.6 118.0 %copy-start.14 = (f32[128,128]{1,0:T(8,128)S(1)}, f32[128,128]{1,0:T(8,128)}, u32[]{:S(2)}) copy-start(f32[128,128]{1,0:T(8,128)} %param.19) | copy-start | bytes 196612
  442.2 111.6 %copy-start.2 = (f32[512,128]{0,1:T(8,128)S(1)}, f32[512,128]{0,1:T(8,128)}, u32[]{:S(2)}) copy-start(f32[512,128]{0,1:T(8,128)} %copy-done.1) | copy-start | bytes 786436
  442.2 111.6 %copy-start.13 = (f32[2,128,128]{2,1,0:T(8,128)S(1)}, f32[2,128,128]{2,1,0:T(8,128)}, u32[]{:S(2)}) copy-start(f32[2,128,128]{2,1,0:T(8,128)} %param.18) | copy-start | bytes 393220
  550.5 618.3 %reduce-scatter.5.cloned.1.call-start = ((), (), s32[]{:S(2)}) async-start(), calls=%async_computation.3 | async-start | bytes 294912 | tf_op jit(solution)/shard_map/reduce_scatter | solution.py:150
  552.5 656.5 %reduce-scatter.3.cloned.1.call-start = ((), (), s32[]{:S(2)}) async-start(), calls=%async_computation.2 | async-start | bytes 294912 | tf_op jit(solution)/shard_map/reduce_scatter | solution.py:149
Sparse Core Ops, SparseCore 0:
  12.0 160.5 all-gather.8
  282.7 151.7 all-gather.10
  438.0 255.7 all-reduce.2
  699.7 435.8 all-reduce.4
  1139.0 29.7 reduce-scatter.4
  1172.0 36.9 reduce-scatter.2
where the time goes:
time: 1220 us
  waiting for transfers between devices  740 us (61%)
  blocking collectives  168 us (14%)
  other arithmetic  133 us (11%)
  local copies, waits for them, and re-layouts  116 us (10%)
  matrix products  40.1 us (3%)
  between operations  14.6 us (1%)
    psum x1, waiting for transfers between devices, on_device(): grad_kweight = lax.psum(grad_kweight, ('ctx', 'head'))  440 us
    all_gather x2, blocking collectives, entering(): pieces = jax.tree.map(lambda part: lax.all_gather(part, axis), value)  168 us
    psum x1, waiting for transfers between devices, on_device(): grad_qweight = lax.psum(jnp.stack(weight_grads, axis=0), 'ctx')  138 us
    select_n x252, other arithmetic, turn(): jnp.where(position < mine, new, old)  121 us
    all_gather x2, waiting for transfers between devices, entering(): pieces = jax.tree.map(lambda part: lax.all_gather(part, axis), value)  90.2 us
    dynamic_slice x126, local copies, waits for them, and re-layouts, turn(): longer = join(total, jax.tree.map(lambda part: part[position], pieces))  89 us
    reduce_scatter x1, waiting for transfers between devices, on_device(): lax.psum_scatter(grad_key_part, 'head', scatter_dimension=0, tiled=True)  40.2 us
    reduce_scatter x1, waiting for transfers between devices, on_device(): lax.psum_scatter(grad_vals, 'head', scatter_dimension=0, tiled=True)  31.7 us
  transfers between devices with their start and end apart: 6, of which 6 were waited for; matrix products, arithmetic and copies ran while one was open for 14% of the time, Pallas kernels for 0%

commit v1 on v0

--- a/solution.py
+++ b/solution.py
@@ -149,7 +149,7 @@
         lax.psum_scatter(grad_key_part, "head", scatter_dimension=0, tiled=True),
         lax.psum_scatter(grad_vals, "head", scatter_dimension=0, tiled=True),
     )
-    grad_qweight = lax.psum(jnp.stack(weight_grads, axis=0), "ctx")
+    grad_qweight = jnp.sum(lax.all_gather(jnp.stack(weight_grads, axis=0), "ctx"), axis=0)
     grad_kweight = lax.psum(grad_kweight, ("ctx", "head"))
     return (
         jnp.concatenate(query_grads, axis=1),

time: 1220 us -> 1120 us (0.918)
  waiting for transfers between devices: 740 us -> 630 us
    psum x1 -> x0, waiting for transfers between devices: 138 us -> none  [on_device(): grad_qweight = lax.psum(jnp.stack(weight_grads, axis=0), 'ctx')]
    all_gather x0 -> x1, waiting for transfers between devices: none -> 33.8 us  [on_device(): lax.all_gather(jnp.stack(weight_grads, axis=0), 'ctx')]
  transfers between devices with their start and end apart: 6 -> 6, of which waited for: 6 -> 6; matrix products, arithmetic and copies ran while one was open for 14% -> 16% of each run, Pallas kernels for 0% -> 0%
where the time goes in v1:
time: 1120 us; the launch traced here: 1110 us
  waiting for transfers between devices  630 us (56%)
  blocking collectives  168 us (15%)
  other arithmetic  139 us (12%)
  local copies, waits for them, and re-layouts  114 us (10%)
  matrix products  43.3 us (4%)
  between operations  14.7 us (1%)
    psum x1, waiting for transfers between devices, on_device(): grad_kweight = lax.psum(grad_kweight, ('ctx', 'head'))  437 us
    all_gather x2, blocking collectives, entering(): pieces = jax.tree.map(lambda part: lax.all_gather(part, axis), value)  168 us
    select_n x252, other arithmetic, turn(): jnp.where(position < mine, new, old)  121 us
    dynamic_slice x126, local copies, waits for them, and re-layouts, turn(): longer = join(total, jax.tree.map(lambda part: part[position], pieces))  89.1 us
    all_gather x2, waiting for transfers between devices, entering(): pieces = jax.tree.map(lambda part: lax.all_gather(part, axis), value)  87.2 us
    reduce_scatter x1, waiting for transfers between devices, on_device(): lax.psum_scatter(grad_key_part, 'head', scatter_dimension=0, tiled=True)  40.2 us
    all_gather x1, waiting for transfers between devices, on_device(): lax.all_gather(jnp.stack(weight_grads, axis=0), 'ctx')  33.8 us
    dot_general x25, matrix products, product(): jnp.einsum(form, left, right, precision=lax.Precision.HIGHEST, preferred_...  32.9 us
  transfers between devices with their start and end apart: 6, of which 6 were waited for; matrix products, arithmetic and copies ran while one was open for 16% of the time, Pallas kernels for 0%

profile of v1, /device:TPU:2, one launch (start us, length us, event | category | flops | bytes accessed | tf_op | source)
XLA Modules:
  0.0 1113.4 jit_solution(2401626741103943695)
XLA Ops:
  7.3 1.5 fusion.97
  9.1 2.1 fusion.103
  12.0 1.2 slice_multiply_fusion.1
  14.2 87.9 %all-gather.5 = f32[64,1,256]{2,1,0:T(1,128)S(1)} all-gather(f32[1,1,256]{2,1,0:T(1,128)S(1)} %bitcast.228), channel_id=3, replica_groups=mesh['ctx'=64,'head'=8] {'ctx'}, dimensions={0}, use_global_device_ids=true | all-gather | bytes 66560 | tf_op jit(solution)/shard_map/all_gather | solution.py:9
  105.4 1.8 fusion.102
  107.2 1.8 fusion.104
  109.0 62.9 %all-gather.11.cloned.1.call-done = f32[16384,128]{1,0:T(8,128)} async-done(((f32[256,128]{1,0:T(8,128)}), f32[16384,128]{1,0:T(8,128)}) %all-gather.11.cloned.1.call-update) | async-done | bytes 8388624 | tf_op jit(solution)/shard_map/all_gather | solution.py:9
  171.9 106.4 %while.32 = (s32[]{:T(128)}, f32[256,128]{1,0:T(8,128)S(1)}, f32[256]{0:T(256)S(1)}, s32[]{:T(128)}, f32[64,256,128]{2,1,0:T(8,128)}, /*index=5*/f32[64,256]{1,0:T(8,128)}, s32[]{:T(128)}, s32[]{:T(128)}) while((s32[]{:T(128)}, f32[256,128]{1,0:T(8,128)S(1)}, f32[256]{0:T(256)S(1)}, s32[]{:T(128)}, f32[64,256,128]{2,1,0:T(8,128)}, ...), condition=%wide.region_15.16_spmd.clone, body=%wide.region_14.15_spmd.clone.sunk | while | flops 99076 | bytes 398459 | solution.py:21
  278.3 1.0 subtract_add_fusion
  280.2 1.6 fusion.35
  281.8 2.1 fusion.105
  284.3 1.3 fusion
  285.6 1.1 fusion.19
  286.6 1.6 fusion.14
  288.2 1.1 fusion.39
  289.3 1.6 fusion.15
  293.3 80.1 %all-gather.6 = f32[64,1,256]{2,1,0:T(1,128)S(1)} all-gather(f32[1,1,256]{2,1,0:T(1,128)S(1)} %bitcast.227), channel_id=5, replica_groups=mesh['ctx'=64,'head'=8] {'ctx'}, dimensions={0}, use_global_device_ids=true | all-gather | bytes 66560 | tf_op jit(solution)/shard_map/all_gather | solution.py:9
  374.1 1.3 fusion.9
  376.7 1.3 fusion.5
  378.9 1.8 copy.217
  380.7 1.8 copy.218
  382.5 1.4 fusion.11
  385.2 1.6 fusion.6
  389.2 1.5 fusion.44
  390.7 1.1 reduce-window_subtract_fusion
  391.8 1.5 convolution_add_fusion.2
  393.4 1.4 fusion.4
  394.8 2.1 copy.211
  396.9 1.8 copy.216
  398.7 1.1 multiply_reduce_fusion.2
  399.8 1.1 multiply_subtract_fusion.1
  400.9 1.4 convolution_bitcast_fusion.2
  402.4 1.1 multiply_reduce_fusion.4
  403.5 1.1 multiply_subtract_fusion.2
  404.6 1.3 convolution_bitcast_fusion.3
  406.8 1.7 fusion.93
  408.5 1.0 fusion.27
  409.5 2.3 fusion.7
  411.9 24.2 %all-gather.13.cloned.1.call-done = f32[16384,128]{1,0:T(8,128)} async-done(((f32[256,128]{1,0:T(8,128)}), f32[16384,128]{1,0:T(8,128)}) %all-gather.13.cloned.1.call-update) | async-done | bytes 8388624 | tf_op jit(solution)/shard_map/all_gather | solution.py:9
  436.2 7.7 rev.6
  443.9 106.5 %while.33 = (s32[]{:T(128)}, f32[256,128]{1,0:T(8,128)S(1)}, f32[256]{0:T(256)S(1)}, s32[]{:T(128)}, f32[64,256,128]{2,1,0:T(8,128)}, /*index=5*/f32[64,256]{1,0:T(8,128)}, s32[]{:T(128)}, s32[]{:T(128)}) while((s32[]{:T(128)}, f32[256,128]{1,0:T(8,128)S(1)}, f32[256]{0:T(256)S(1)}, s32[]{:T(128)}, f32[64,256,128]{2,1,0:T(8,128)}, ...), condition=%wide.region_33.34_spmd.clone, body=%wide.region_32.33_spmd.clone.sunk | while | flops 99076 | bytes 398459 | solution.py:21
  451.4 0.9 add_select_fusion.10
  461.5 0.9 add_select_fusion.10
  490.2 0.9 add_select_fusion.10
  495.3 0.9 add_select_fusion.10
  498.7 0.9 add_select_fusion.10
  522.3 1.0 add_select_fusion.10
  530.8 0.9 add_select_fusion.10
  534.1 0.9 add_select_fusion.10
  535.8 1.0 add_select_fusion.10
  539.2 0.9 add_select_fusion.10
  542.6 0.9 add_select_fusion.10
  546.0 0.9 add_select_fusion.10
  547.7 0.9 add_select_fusion.10
  551.1 1.0 convolution_bitcast_fusion.1
  552.5 1.7 convolution_add_fusion.5
  554.2 1.3 fusion.106
  556.4 1.0 copy.182
  557.4 33.8 %all-gather.15.cloned.1.call-done = f32[128,128,128]{2,1,0:T(8,128)} async-done(((f32[2,128,128]{2,1,0:T(8,128)}), f32[128,128,128]{2,1,0:T(8,128)}) %all-gather.15.cloned.1.call-update) | async-done | bytes 8388624 | tf_op jit(solution)/shard_map/all_gather | solution.py:152
  591.2 4.4 reduce_sum.229
  595.6 437.5 %all-reduce.2.cloned.1.call-done = f32[128,128]{0,1:T(8,128)} async-done(((f32[128,128]{0,1:T(8,128)}), f32[128,128]{0,1:T(8,128)}) %all-reduce.2.cloned.1.call-update) | async-done | bytes 65552 | tf_op jit(solution)/shard_map/psum | solution.py:153
  1033.1 1.6 copy.184
  1034.7 31.7 %reduce-scatter.5.cloned.1.call-done = f32[64,128]{1,0:T(8,128)} async-done(((f32[512,128]{1,0:T(8,128)}), f32[64,128]{1,0:T(8,128)}) %reduce-scatter.5.cloned.1.call-update) | async-done | bytes 32784 | tf_op jit(solution)/shard_map/reduce_scatter | solution.py:150
  1066.3 40.2 %reduce-scatter.3.cloned.1.call-done = f32[64,128]{1,0:T(8,128)} async-done(((f32[512,128]{1,0:T(8,128)}), f32[64,128]{1,0:T(8,128)}) %reduce-scatter.3.cloned.1.call-update) | async-done | bytes 32784 | tf_op jit(solution)/shard_map/reduce_scatter | solution.py:149
  (464 shorter events, 215.8 us)
Async XLA Ops:
  7.2 1.9 copy-start
  7.2 96.9 %copy-start.11 = (f32[2,128,128]{2,1,0:T(8,128)S(1)}, f32[2,128,128]{2,1,0:T(8,128)}, u32[]{:S(2)}) copy-start(f32[2,128,128]{2,1,0:T(8,128)} %param.18) | copy-start | bytes 393220
  7.2 96.9 %copy-start.3 = (f32[512,256]{1,0:T(8,128)S(1)}, f32[512,256]{1,0:T(8,128)}, u32[]{:S(2)}) copy-start(f32[512,256]{1,0:T(8,128)} %param.12) | copy-start | bytes 1572868
  7.2 164.7 %all-gather.11.cloned.1.call-start = ((), (), s32[]{:S(2)}) async-start(), calls=%async_computation.5 | async-start | bytes 8519680 | tf_op jit(solution)/shard_map/all_gather | solution.py:9
  11.1 425.0 %all-gather.13.cloned.1.call-start = ((), (), s32[]{:S(2)}) async-start(), calls=%async_computation.6 | async-start | bytes 8519680 | tf_op jit(solution)/shard_map/all_gather | solution.py:9
  104.1 3.1 copy-start.10
  280.2 10.7 copy-start.15
  283.9 307.3 %all-gather.15.cloned.1.call-start = ((), (), s32[]{:S(2)}) async-start(), calls=%async_computation.7 | async-start | bytes 8519680 | tf_op jit(solution)/shard_map/all_gather | solution.py:152
  288.2 102.5 %copy-start.5 = (f32[256,128]{1,0:T(8,128)S(1)}, f32[256,128]{1,0:T(8,128)}, u32[]{:S(2)}) copy-start(f32[256,128]{1,0:T(8,128)} %get-tuple-element.355) | copy-start | bytes 393220
  290.9 2.4 copy-start.14
  292.7 0.6 copy-start.18
  373.4 11.8 %copy-start.16 = (f32[4,128]{1,0:T(4,128)S(1)}, f32[4,128]{1,0:T(4,128)}, u32[]{:S(2)}) copy-start(f32[4,128]{1,0:T(4,128)} %copy-done.15) | copy-start | bytes 6148
  375.4 0.7 copy-start.6
  383.9 0.7 copy-start.7
  386.9 19.9 %copy-start.17 = (f32[4,128]{1,0:T(4,128)S(1)}, f32[4,128]{1,0:T(4,128)}, u32[]{:S(2)}) copy-start(f32[4,128]{1,0:T(4,128)} %copy-done.15) | copy-start | bytes 6148
  400.9 3.7 copy-start.1
  411.9 621.2 %all-reduce.2.cloned.1.call-start = ((), (), s32[]{:S(2)}) async-start(), calls=%async_computation.4 | async-start | bytes 131072 | tf_op jit(solution)/shard_map/psum | solution.py:153
  436.2 114.2 %copy-start.4 = (f32[512,256]{0,1:T(8,128)S(1)}, f32[512,256]{0,1:T(8,128)}, u32[]{:S(2)}) copy-start(f32[512,256]{0,1:T(8,128)} %copy.211) | copy-start | bytes 1572868
  436.2 115.0 %copy-start.8 = (f32[512,128]{1,0:T(8,128)S(1)}, f32[512,128]{1,0:T(8,128)}, u32[]{:S(2)}) copy-start(f32[512,128]{1,0:T(8,128)} %param.13) | copy-start | bytes 786436
  436.2 116.3 %copy-start.9 = (f32[4,128,128]{2,1,0:T(8,128)S(1)}, f32[4,128,128]{2,1,0:T(8,128)}, u32[]{:S(2)}) copy-start(f32[4,128,128]{2,1,0:T(8,128)} %fusion.7) | copy-start | bytes 786436
  436.2 118.1 %copy-start.13 = (f32[128,128]{1,0:T(8,128)S(1)}, f32[128,128]{1,0:T(8,128)}, u32[]{:S(2)}) copy-start(f32[128,128]{1,0:T(8,128)} %param.19) | copy-start | bytes 196612
  443.9 111.7 %copy-start.2 = (f32[512,128]{0,1:T(8,128)S(1)}, f32[512,128]{0,1:T(8,128)}, u32[]{:S(2)}) copy-start(f32[512,128]{0,1:T(8,128)} %copy-done.1) | copy-start | bytes 786436
  443.9 111.7 %copy-start.12 = (f32[2,128,128]{2,1,0:T(8,128)S(1)}, f32[2,128,128]{2,1,0:T(8,128)}, u32[]{:S(2)}) copy-start(f32[2,128,128]{2,1,0:T(8,128)} %param.18) | copy-start | bytes 393220
  552.2 514.2 %reduce-scatter.5.cloned.1.call-start = ((), (), s32[]{:S(2)}) async-start(), calls=%async_computation.3 | async-start | bytes 294912 | tf_op jit(solution)/shard_map/reduce_scatter | solution.py:150
  554.2 552.4 %reduce-scatter.3.cloned.1.call-start = ((), (), s32[]{:S(2)}) async-start(), calls=%async_computation.2 | async-start | bytes 294912 | tf_op jit(solution)/shard_map/reduce_scatter | solution.py:149
Sparse Core Ops, SparseCore 0:
  11.3 160.5 all-gather.10
  284.1 152.0 all-gather.12
  439.1 152.0 all-gather.14
  597.1 435.9 all-reduce.1
  1036.5 29.7 reduce-scatter.4
  1069.6 36.9 reduce-scatter.2
